TPU v7x, 32 devices: a whole 2x2x4 slice. The times are simulated.
32 devices in a mesh: seq: 8 (over z, x), dp: 4 (over y, core).
Axes of the slice: x: 2, y: 2, z: 4, core: 2. Of those that a mesh axis runs over, the one named last changes fastest.
Arguments:
- linear_queries: bfloat16 [4, 1024, 2048], P('dp', 'seq'), may hold values from -6 to 6
- linear_keys: bfloat16 [4, 1024, 2048], P('dp', 'seq'), may hold values from -6 to 6
- window_queries: bfloat16 [4, 1024, 2048], P('dp', 'seq'), may hold values from -41 to 41
- window_keys: bfloat16 [4, 1024, 2048], P('dp', 'seq'), may hold values from -12 to 12
- values: bfloat16 [4, 1024, 2048], P('dp', 'seq'), may hold values from -8 to 8
- cotangent: bfloat16 [4, 1024, 2048], P('dp', 'seq'), may hold values from -10 to 10
- feature_map: bfloat16 [16, 128, 128], replicated, may hold values from -0.5 to 0.5
Outputs:
- attended: bfloat16 [4, 1024, 2048], P('dp', 'seq')
- dlinear_queries: bfloat16 [4, 1024, 2048], P('dp', 'seq')
- dlinear_keys: bfloat16 [4, 1024, 2048], P('dp', 'seq')
- dwindow_queries: bfloat16 [4, 1024, 2048], P('dp', 'seq')
- dwindow_keys: bfloat16 [4, 1024, 2048], P('dp', 'seq')
- dvalues: bfloat16 [4, 1024, 2048], P('dp', 'seq')
- dfeature_map: float32 [16, 128, 128], replicated
All inputs are finite; a program needn't handle non-finite values.
Results may differ from a plain program's by a relative error of at most 0.009.
Values may be sent and summed in bfloat16 or wider, within the bound.
No kernel may reach another device: no remote copies, remote signals or barrier semaphores. Data moves between devices by JAX's collectives and lax.ppermute only.
A program may use at most 192 MiB of HBM per device.

v0:
```python
import jax
import jax.numpy as jnp
from jax import lax
from jax.sharding import PartitionSpec as P

HEADS = 16
HD = 128
WINDOW = 64


def entering(shard, axis, join, neutral, backward):
    count = lax.axis_size(axis)
    place = lax.axis_index(axis)
    ahead = count - 1 - place if backward else place
    gathered = lax.all_gather(shard.astype(jnp.bfloat16), axis)
    state = jnp.zeros_like(shard) + jnp.asarray(neutral, shard.dtype)

    def one(turn, state):
        source = count - 1 - turn if backward else turn
        return join(state, lax.dynamic_index_in_dim(gathered, source, 0, False).astype(shard.dtype))

    return lax.fori_loop(0, ahead, one, state)


def passed_along(block, axis, distance):
    devices = range(lax.axis_size(axis))
    route = [(i - distance, i) for i in devices if i - distance in devices]
    return lax.ppermute(block, axis, route)


def plain(form, left, right):
    return jnp.einsum(form, left, right, preferred_element_type=jnp.float32)


def exact(form, left, right):
    return jnp.einsum(
        form, left.astype(jnp.float32), right.astype(jnp.float32), precision=lax.Precision.HIGHEST
    )


def feature(inputs, feature_map):
    before = plain("htd,hde->hte", inputs, feature_map)
    mapped = jnp.where(before > 0, before + 1.0, jnp.exp(jnp.minimum(before, 0.0)))
    return (before, mapped.astype(jnp.bfloat16))


def slope(before):
    return jnp.where(before > 0, 1.0, jnp.exp(jnp.minimum(before, 0.0)))


def split_heads(matrix):
    return matrix.reshape(matrix.shape[0], HEADS, HD).transpose(1, 0, 2)


def join_heads(tensor):
    return tensor.transpose(1, 0, 2).reshape(tensor.shape[1], HEADS * HD)


def exclusive(terms, reverse):
    zero = jnp.zeros_like(terms[:1])
    if reverse:
        totals = jnp.flip(jnp.cumsum(jnp.flip(terms, 0), axis=0), 0)
        return jnp.concatenate([totals[1:], zero], axis=0)
    totals = jnp.cumsum(terms, axis=0)
    return jnp.concatenate([zero, totals[:-1]], axis=0)


def band_mask():
    rows = lax.broadcasted_iota(jnp.int32, (WINDOW, 2 * WINDOW), 0)
    cols = lax.broadcasted_iota(jnp.int32, (WINDOW, 2 * WINDOW), 1)
    offset = cols - rows
    return (offset >= 1) & (offset <= WINDOW)


def window_mask(blocks, start):
    cols = lax.broadcasted_iota(jnp.int32, (blocks, WINDOW, 2 * WINDOW), 2)
    block = lax.broadcasted_iota(jnp.int32, (blocks, WINDOW, 2 * WINDOW), 0)
    keypos = start + block * WINDOW + cols - WINDOW
    return band_mask()[None] & (keypos >= 0)


def causal_mask():
    rows = lax.broadcasted_iota(jnp.int32, (WINDOW, WINDOW), 0)
    cols = lax.broadcasted_iota(jnp.int32, (WINDOW, WINDOW), 1)
    return rows >= cols


def pairs(rim, inputs):
    blocks = inputs.shape[1] // WINDOW
    early = jnp.concatenate([rim, inputs[:, : inputs.shape[1] - WINDOW]], axis=1).reshape(
        HEADS, blocks, WINDOW, HD
    )
    late = inputs.reshape(HEADS, blocks, WINDOW, HD)
    return jnp.concatenate([early, late], axis=2)


def softmax_rows(score, mask):
    top = jnp.max(jnp.where(mask, score, -jnp.inf), axis=-1, keepdims=True)
    expo = jnp.exp(jnp.where(mask, score - top, -jnp.inf))
    return expo / jnp.sum(expo, axis=-1, keepdims=True)


def fold_pairs(pair, rim):
    after = jnp.concatenate([pair[:, 1:, :WINDOW], rim[:, None]], axis=1)
    return pair[:, :, WINDOW:] + after


def add_up(earlier, later):
    return earlier + later


def carry_states(totals, reverse):
    if reverse:
        return entering(totals, "seq", add_up, jnp.zeros_like(totals), True)
    return entering(totals, "seq", add_up, jnp.zeros_like(totals), False)


def on_device(
    linear_queries, linear_keys, window_queries, window_keys, values, cotangent, feature_map
):
    tokens = linear_queries.shape[1]
    blocks = tokens // WINDOW
    block_shape = (HEADS, blocks, WINDOW, HD)
    length = tokens * lax.axis_size("seq")
    lin_scale = 1.0 / (HD * length)
    inverse_root = HD ** (-0.5)
    win_heads = split_heads(window_queries[0])
    wkey_heads = split_heads(window_keys[0])
    value_heads = split_heads(values[0])
    grad_full = split_heads(cotangent[0])
    key_rim, value_rim = passed_along(
        (wkey_heads[:, tokens - WINDOW :], value_heads[:, tokens - WINDOW :]), "seq", 1
    )
    query_heads = split_heads(linear_queries[0])
    key_heads = split_heads(linear_keys[0])
    pre_query, feat_query = feature(query_heads, feature_map)
    pre_key, feat_key = feature(key_heads, feature_map)
    query_blocks = feat_query.reshape(block_shape)
    key_blocks = feat_key.reshape(block_shape)
    value_blocks = value_heads.reshape(block_shape)
    causal = causal_mask()
    lin_scores = jnp.where(causal, plain("hncf,hnsf->hncs", query_blocks, key_blocks), 0.0)
    block_states = plain("hnsf,hnsd->nhfd", key_blocks, value_blocks)
    state_in = carry_states(jnp.sum(block_states, axis=0), False)[None] + exclusive(
        block_states, False
    )
    lin = (
        exact("hncs,hnsd->hncd", lin_scores, value_blocks)
        + exact("hncf,nhfd->hncd", query_blocks, state_in)
    ) * lin_scale
    win_queries = win_heads.reshape(block_shape)
    key_pairs = pairs(key_rim, wkey_heads)
    value_pairs = pairs(value_rim, value_heads)
    mask = window_mask(blocks, lax.axis_index("seq") * tokens)
    prob = softmax_rows(plain("hncd,hnsd->hncs", win_queries, key_pairs) * inverse_root, mask[None])
    prob_b = prob.astype(jnp.bfloat16)
    win = plain("hncs,hnsd->hncd", prob_b, value_pairs)
    attended = join_heads((lin + win).astype(jnp.bfloat16).reshape(HEADS, tokens, HD))
    grad_heads = grad_full.reshape(block_shape)
    grad_lin = grad_heads.astype(jnp.float32) * lin_scale
    mixed = jnp.where(causal, plain("hncd,hnsd->hncs", grad_heads, value_blocks), 0.0) * lin_scale
    dfeat_query = exact("hncs,hnsf->hncf", mixed, key_blocks) + exact(
        "hncd,nhfd->hncf", grad_lin, state_in
    )
    grad_states = plain("hncf,hncd->nhfd", query_blocks, grad_heads) * lin_scale
    state_after = carry_states(jnp.sum(grad_states, axis=0), True)[None] + exclusive(
        grad_states, True
    )
    dfeat_key = exact("hncs,hncf->hnsf", mixed, query_blocks) + exact(
        "nhfd,hnsd->hnsf", state_after, value_blocks
    )
    dvalue_lin = exact("hncs,hncd->hnsd", lin_scores, grad_lin) + exact(
        "hnsf,nhfd->hnsd", key_blocks, state_after
    )
    dpre_query = (dfeat_query.reshape(HEADS, tokens, HD) * slope(pre_query)).astype(jnp.bfloat16)
    dpre_key = (dfeat_key.reshape(HEADS, tokens, HD) * slope(pre_key)).astype(jnp.bfloat16)
    dlin_queries = join_heads(plain("htf,hdf->htd", dpre_query, feature_map).astype(jnp.bfloat16))
    dlin_keys = join_heads(plain("htf,hdf->htd", dpre_key, feature_map).astype(jnp.bfloat16))
    map_terms = plain("htd,hte->hde", query_heads, dpre_query) + plain(
        "htd,hte->hde", key_heads, dpre_key
    )
    dprob = plain("hncd,hnsd->hncs", grad_heads, value_pairs)
    delta = jnp.sum(prob * dprob, axis=-1, keepdims=True)
    dscore = (prob * (dprob - delta) * inverse_root).astype(jnp.bfloat16)
    dwin_queries = join_heads(
        plain("hncs,hnsd->hncd", dscore, key_pairs).reshape(HEADS, tokens, HD).astype(jnp.bfloat16)
    )
    key_pair_grads = plain("hncs,hncd->hnsd", dscore, win_queries)
    value_pair_grads = plain("hncs,hncd->hnsd", prob_b, grad_heads)
    rim_keys, rim_values = (
        passed_along(key_pair_grads[:, 0, :WINDOW].astype(jnp.bfloat16), "seq", -1).astype(
            jnp.float32
        ),
        passed_along(value_pair_grads[:, 0, :WINDOW].astype(jnp.bfloat16), "seq", -1).astype(
            jnp.float32
        ),
    )
    dkey_win = fold_pairs(key_pair_grads, rim_keys)
    dvalue_win = fold_pairs(value_pair_grads, rim_values)
    dwin_keys = join_heads(dkey_win.reshape(HEADS, tokens, HD).astype(jnp.bfloat16))
    dvalue_all = join_heads(
        (dvalue_lin + dvalue_win).reshape(HEADS, tokens, HD).astype(jnp.bfloat16)
    )
    total_tokens = length * lax.axis_size("dp") * linear_queries.shape[0]
    map_grad = lax.psum(map_terms, ("seq", "dp")) * total_tokens ** (-0.5)
    return (
        attended[None],
        dlin_queries[None],
        dlin_keys[None],
        dwin_queries[None],
        dwin_keys[None],
        dvalue_all[None],
        map_grad,
    )


def solution(mesh):
    return jax.shard_map(
        on_device,
        mesh=mesh,
        in_specs=(
            P("dp", "seq", None),
            P("dp", "seq", None),
            P("dp", "seq", None),
            P("dp", "seq", None),
            P("dp", "seq", None),
            P("dp", "seq", None),
            P(),
        ),
        out_specs=(
            P("dp", "seq", None),
            P("dp", "seq", None),
            P("dp", "seq", None),
            P("dp", "seq", None),
            P("dp", "seq", None),
            P("dp", "seq", None),
            P(),
        ),
        check_vma=False,
    )
```

profile of v0, /device:TPU:0, one launch (start us, length us, event | category | flops | bytes accessed | tf_op | source)
XLA Modules:
  0.0 374.6 jit_solution(10899480268621206970)
XLA Ops:
  7.2 1.2 copy.141
  8.4 1.3 copy.140
  10.4 2.8 multiply_reduce_fusion
  13.3 3.2 reverse.4
  17.7 1.3 fusion.57
  19.0 1.4 fusion.34
  20.4 69.1 %all-gather.7.cloned.1.call-done = bf16[128,128,128]{2,1,0:T(8,128)(2,1)} async-done(((bf16[16,128,128]{2,1,0:T(8,128)(2,1)}), bf16[128,128,128]{2,1,0:T(8,128)(2,1)}) %all-gather.7.cloned.1.call-update) | async-done | bytes 4194320 | tf_op jit(solution)/shard_map/all_gather | solution.py:15
  89.6 9.2 %while.23 = (s32[]{:T(128)}, f32[16,128,128]{2,1,0:T(8,128)S(1)}, s32[]{:T(128)}, bf16[8,16,128,128]{3,2,1,0:T(8,128)(2,1)}, s32[]{:T(128)}, /*index=5*/s32[]{:T(128)}, s32[]{:T(128)}, s32[]{:T(128)}) while((s32[]{:T(128)}, f32[16,128,128]{2,1,0:T(8,128)S(1)}, s32[]{:T(128)}, bf16[8,16,128,128]{3,2,1,0:T(8,128)(2,1)}, s32[]{:T(128)}, ...), condition=%wide.region_8.9_spmd, body=%wide.region_7.8_spmd.sunk | while | flops 524294 | bytes 2621575 | solution.py:22
  89.6 1.3 convert_add_fusion.5
  90.9 1.3 convert_add_fusion.5
  92.2 1.3 convert_add_fusion.5
  93.5 1.3 convert_add_fusion.5
  94.8 1.3 convert_add_fusion.5
  96.2 1.3 convert_add_fusion.5
  97.5 1.3 convert_add_fusion.5
  98.8 2.0 select_add_fusion
  100.8 2.3 fusion.14
  103.1 1.0 convolution_add_fusion.2
  105.3 2.8 fusion.112
  108.1 1.1 copy.138
  111.0 2.0 collective-permute-start
  113.7 2.2 collective-permute-start.1
  116.0 1.2 copy.139
  117.4 7.1 %collective-permute-done = bf16[16,64,128]{2,1,0:T(8,128)(2,1)} collective-permute-done((bf16[16,64,128]{2,1,0:T(8,128)(2,1)}, bf16[16,64,128]{2,1,0:T(8,128)(2,1)}, u32[]{:S(2)}, u32[]{:S(2)}) %collective-permute-start) | collective-permute-done | bytes 262176 | tf_op jit(solution)/shard_map/ppermute | solution.py:28
  124.6 1.0 pad_maximum_fusion.6
  125.6 2.9 collective-permute-done.1
  128.5 1.0 pad_maximum_fusion.7
  129.5 1.8 convolution_bitcast_fusion
  133.1 1.4 fusion.113
  134.5 15.4 %fusion.51 = f32[16,2,128,128]{3,2,1,0:T(8,128)} fusion(bf16[16,2,64,128]{3,2,1,0:T(8,128)(2,1)} %bitcast.171, f32[16,2,64,128]{3,2,1,0:T(8,128)} %convolution_bitcast_fusion, f32[16,2,64,128]{3,2,1,0:T(8,128)} %get-tuple-element.151, f32[16,2,64]{2,1,0:T(2,128)S(1)} %get-tuple-element.150), kind=kOutput, calls=%fused_computation.71 | convolution fusion | flops 68946048 | bytes 4726784 | tf_op jit(solution)/shard_map/hncs,hncd->hnsd/dot_general | solution.py:32
  149.9 1.8 fusion.81
  151.7 1.5 collective-permute-start.2
  153.2 7.1 %fusion.83 = f32[16,2,128,128]{3,2,1,0:T(8,128)} fusion(bf16[16,2,64,128]{3,2,1,0:T(8,128)(2,1)S(1)} %bitcast.154, f32[16,2,64]{2,1,0:T(2,128)S(1)} %get-tuple-element.150, f32[16,2,64,128]{3,2,1,0:T(8,128)} %copy-done.20, pred[2,64,128]{2,1,0:T(8,128)(4,1)S(1)} %fusion.86), kind=kOutput, calls=%fused_computation.111 | convolution fusion | flops 68421760 | bytes 3694592 | tf_op jit(solution)/shard_map/hncs,hncd->hnsd/dot_general | solution.py:32
  160.2 1.8 fusion.82
  162.0 14.3 %convolution_convert_fusion.2 = bf16[16,2,64,128]{3,2,1,0:T(8,128)(2,1)} fusion(f32[16,2,64,128]{3,2,1,0:T(8,128)} %convolution_bitcast_fusion, bf16[16,2,64,128]{3,2,1,0:T(8,128)(2,1)} %bitcast.160, bf16[16,2,64,128]{3,2,1,0:T(8,128)(2,1)} %bitcast.173, f32[16,2,64,128]{3,2,1,0:T(8,128)} %get-tuple-element.151, f32[16,2,64]{2,1,0:T(2,128)S(1)} %get-tuple-element.150), kind=kOutput, calls=%fused_computation.43 | convolution fusion | flops 71305344 | bytes 3678208 | tf_op jit(solution)/shard_map/hncs,hnsd->hncd/dot_general | solution.py:32
  176.4 1.9 slice.58
  178.3 1.3 collective-permute-start.3
  179.6 2.2 copy.114
  181.7 2.1 broadcast_in_dim_reshape.21
  183.8 1.1 slice_bitcast_fusion
  184.9 1.0 bitcast_convert_fusion.1
  185.9 1.4 fusion.49
  188.1 2.0 copy.118
  190.2 2.0 copy.127
  192.3 1.8 fusion.114
  194.0 1.1 slice.49
  196.0 1.1 fusion.4
  198.1 1.9 fusion.48
  200.1 1.1 copy.122
  201.2 2.1 broadcast_in_dim_reshape.23
  203.3 1.3 convolution_convert_fusion
  204.6 2.0 copy.126
  206.6 2.8 fusion.115
  209.8 5.7 %fusion.17 = f32[16,2,64,128]{3,2,1,0:T(8,128)S(1)} fusion(f32[16,2,64,128]{3,2,1,0:T(8,128)} %fusion.115, bf16[16,2,64,128]{3,2,1,0:T(8,128)(2,1)S(1)} %bitcast.156, f32[1,16,128,128]{3,2,1,0:T(8,128)} %slice.49, f32[16,128,128]{2,1,0:T(8,128)S(1)} %get-tuple-element.86), kind=kOutput, calls=%fused_computation.20 | convolution fusion | flops 403963904 | bytes 4718592 | tf_op jit(solution)/shard_map/hncd,nhfd->hncf/dot_general | solution.py:36
  216.9 1.3 convolution_convert_fusion.1
  218.2 2.1 fusion.10
  220.4 1.4 fusion.31
  221.8 1.0 copy.125
  222.8 2.9 fusion.33
  225.7 5.6 %fusion.35 = bf16[16,2,64,128]{3,2,1,0:T(8,128)(2,1)S(1)} fusion(f32[16,2,64,128]{3,2,1,0:T(8,128)} %fusion.33, bf16[16,2,64,128]{3,2,1,0:T(8,128)(2,1)S(1)} %bitcast.143, bf16[16,2,64,128]{3,2,1,0:T(8,128)(2,1)S(1)} %bitcast.169, f32[16,2,64]{2,1,0:T(2,128)S(1)} %get-tuple-element.150, f32[16,2,64,128]{3,2,1,0:T(8,128)} %copy-done.20, ...), kind=kOutput, calls=%fused_computation.40 | convolution fusion | flops 71043200 | bytes 3694592 | tf_op jit(solution)/shard_map/hncs,hnsd->hncd/dot_general | solution.py:32
  231.7 1.0 broadcast_in_dim_reshape.18
  232.7 132.8 %all-reduce.3.cloned.1.call-done = f32[16,128,128]{1,2,0:T(8,128)} async-done(((f32[16,128,128]{1,2,0:T(8,128)}), f32[16,128,128]{1,2,0:T(8,128)}) %all-reduce.3.cloned.1.call-update) | async-done | bytes 1048592 | tf_op jit(solution)/shard_map/psum | solution.py:205
  365.5 1.3 broadcast_multiply_fusion
  366.8 1.3 copy.128
  (98 shorter events, 12.5 us)
Async XLA Ops:
  7.2 2.6 copy-start
  7.2 82.3 %all-gather.7.cloned.1.call-start = ((), (), s32[]{:S(2)}) async-start(), calls=%async_computation.2 | async-start | bytes 4718592 | tf_op jit(solution)/shard_map/all_gather | solution.py:15
  8.4 1.7 copy-start.15
  10.1 3.1 copy-start.7
  13.2 196.2 %all-gather.5.cloned.1.call-start = ((), (), s32[]{:S(2)}) async-start(), calls=%async_computation.1 | async-start | bytes 4718592 | tf_op jit(solution)/shard_map/all_gather | solution.py:15
  13.3 3.2 copy-start.29
  16.5 1.1 copy-start.30
  16.6 0.8 copy-start.11
  17.7 2.7 copy-start.17
  89.6 9.2 %copy-start.31 = (pred[2]{0:T(512)(128)(4,1)S(1)}, pred[2]{0:T(512)(128)(4,1)}, u32[]{:S(2)}) copy-start(pred[2]{0:T(512)(128)(4,1)} %constant.73.clone.1) | copy-start | bytes 10
  100.8 3.4 copy-start.1
  100.8 2.3 copy-start.5
  103.1 1.2 copy-start.19
  104.2 1.1 copy-start.12
  104.7 98.5 %copy-start.9 = (bf16[16,128,128]{2,1,0:T(8,128)(2,1)}, bf16[16,128,128]{2,1,0:T(8,128)(2,1)S(1)}, u32[]{:S(2)}) copy-start(bf16[16,128,128]{2,1,0:T(8,128)(2,1)S(1)} %get-tuple-element.132) | copy-start | bytes 1572868
  108.0 257.4 %all-reduce.3.cloned.1.call-start = ((), (), s32[]{:S(2)}) async-start(), calls=%async_computation | async-start | bytes 2097152 | tf_op jit(solution)/shard_map/psum | solution.py:205
  109.4 0.8 copy-start.13
  111.0 13.5 %collective-permute-start = (bf16[16,64,128]{2,1,0:T(8,128)(2,1)}, bf16[16,64,128]{2,1,0:T(8,128)(2,1)}, u32[]{:S(2)}, u32[]{:S(2)}) collective-permute-start(bf16[16,64,128]{2,1,0:T(8,128)(2,1)} %get-tuple-element.134), channel_id=1, source_target_pairs={{0,4},{4,8},{8,12},{12,16},{16,20},{20,24},{24,28},{1,5},{5,9},{9,... | collective-permute-start | bytes 786440 | tf_op jit(solution)/shard_map/ppermute | solution.py:28
  113.7 14.8 %collective-permute-start.1 = (bf16[16,64,128]{2,1,0:T(8,128)(2,1)}, bf16[16,64,128]{2,1,0:T(8,128)(2,1)}, u32[]{:S(2)}, u32[]{:S(2)}) collective-permute-start(bf16[16,64,128]{2,1,0:T(8,128)(2,1)} %get-tuple-element.138), channel_id=1, source_target_pairs={{0,4},{4,8},{8,12},{12,16},{16,20},{20,24},{24,28},{1,5},{5,9},{9,... | collective-permute-start | bytes 786440 | tf_op jit(solution)/shard_map/ppermute | solution.py:28
  116.0 8.6 %copy-start.28 = (bf16[16,64,128]{2,1,0:T(8,128)(2,1)S(1)}, bf16[16,64,128]{2,1,0:T(8,128)(2,1)}, u32[]{:S(2)}) copy-start(bf16[16,64,128]{2,1,0:T(8,128)(2,1)} %get-tuple-element.135) | copy-start | bytes 786436
  117.3 14.0 %copy-start.24 = (bf16[16,128,128]{2,1,0:T(8,128)(2,1)}, bf16[16,128,128]{2,1,0:T(8,128)(2,1)S(1)}, u32[]{:S(2)}) copy-start(bf16[16,128,128]{2,1,0:T(8,128)(2,1)S(1)} %copy.106) | copy-start | bytes 1572868
  125.5 6.6 %copy-start.25 = (bf16[16,128,128]{2,1,0:T(8,128)(2,1)}, bf16[16,128,128]{2,1,0:T(8,128)(2,1)S(1)}, u32[]{:S(2)}) copy-start(bf16[16,128,128]{2,1,0:T(8,128)(2,1)S(1)} %pad_maximum_fusion.6) | copy-start | bytes 1572868
  125.6 5.7 %copy-start.14 = (bf16[128,16,128]{2,0,1:T(8,128)(2,1)S(1)}, bf16[128,16,128]{2,0,1:T(8,128)(2,1)}, u32[]{:S(2)}) copy-start(bf16[128,16,128]{2,0,1:T(8,128)(2,1)} %copy-done.13) | copy-start | bytes 1572868
  129.5 1.8 copy-start.21
  132.1 1.0 copy-start.20
  151.7 33.2 %collective-permute-start.2 = (bf16[16,64,128]{2,1,0:T(8,128)(2,1)}, bf16[16,64,128]{2,1,0:T(8,128)(2,1)}, u32[]{:S(2)}, u32[]{:S(2)}) collective-permute-start(bf16[16,64,128]{2,1,0:T(8,128)(2,1)} %fusion.81), channel_id=1, source_target_pairs={{4,0},{8,4},{12,8},{16,12},{20,16},{24,20},{28,24},{5,1},{9,5},{13... | collective-permute-start | bytes 786440 | tf_op jit(solution)/shard_map/ppermute | solution.py:28
  178.3 13.9 %collective-permute-start.3 = (bf16[16,64,128]{2,1,0:T(8,128)(2,1)}, bf16[16,64,128]{2,1,0:T(8,128)(2,1)S(1)}, u32[]{:S(2)}, u32[]{:S(2)}) collective-permute-start(bf16[16,64,128]{2,1,0:T(8,128)(2,1)} %fusion.82), channel_id=1, source_target_pairs={{4,0},{8,4},{12,8},{16,12},{20,16},{24,20},{28,24},{5,1},{9,5},{13... | collective-permute-start | bytes 786440 | tf_op jit(solution)/shard_map/ppermute | solution.py:28
  194.0 2.0 copy-start.2
  196.0 4.1 %copy-start.3 = (f32[16,2,64,64]{3,2,1,0:T(8,128)}, f32[16,2,64,64]{3,2,1,0:T(8,128)S(1)}, u32[]{:S(2)}) copy-start(f32[16,2,64,64]{3,2,1,0:T(8,128)S(1)} %convolution_select_fusion.1) | copy-start | bytes 1572868
  196.0 1.4 copy-start.23
  196.0 2.1 copy-start.27
  209.8 5.7 %copy-start.8 = (f32[16,128,128]{2,1,0:T(8,128)S(1)}, f32[16,128,128]{2,1,0:T(8,128)}, u32[]{:S(2)}) copy-start(f32[16,128,128]{2,1,0:T(8,128)} %copy-done.7) | copy-start | bytes 3145732
  215.5 1.0 copy-start.16
  216.6 1.6 copy-start.6
  218.2 2.1 copy-start.10
  218.2 2.1 copy-start.18
  220.4 1.4 copy-start.26
  220.4 2.4 copy-start.4
  222.8 2.9 copy-start.22
Sparse Core Ops, SparseCore 0:
  13.3 76.0 all-gather.6
  108.2 82.5 all-gather.4
  221.9 143.5 all-reduce.2
where the time goes:
time: 376 us; the launch traced here: 375 us
  waiting for transfers between devices  212 us (56%)
  matrix products  78.2 us (21%)
  local copies, waits for them, and re-layouts  41.8 us (11%)
  other arithmetic  20.9 us (6%)
  between operations  14.3 us (4%)
  starting transfers between devices  7.03 us (2%)
    psum x1, waiting for transfers between devices, on_device(): map_grad = lax.psum(map_terms, ('seq', 'dp')) * total_tokens ** (-0.5)  133 us
    all_gather x2, waiting for transfers between devices, entering(): gathered = lax.all_gather(shard.astype(jnp.bfloat16), axis)  69.1 us
    dot_general x16, matrix products, plain(): return jnp.einsum(form, left, right, preferred_element_type=jnp.float32)  58.2 us
    dot_general x8, matrix products, exact(): jnp.einsum(form, left.astype(jnp.float32), right.astype(jnp.float32), pre...  20 us
    unnamed x75, local copies, waits for them, and re-layouts  18 us
    ppermute x4, waiting for transfers between devices, passed_along(): return lax.ppermute(block, axis, route)  10.1 us
    add x7, other arithmetic, add_up(): return earlier + later  8.98 us
  transfers between devices with their start and end apart: 7, of which 4 were waited for; matrix products, arithmetic and copies ran while one was open for 26% of the time, Pallas kernels for 0%

commit v1 on v0

--- a/solution.py
+++ b/solution.py
@@ -202,7 +202,7 @@
         (dvalue_lin + dvalue_win).reshape(HEADS, tokens, HD).astype(jnp.bfloat16)
     )
     total_tokens = length * lax.axis_size("dp") * linear_queries.shape[0]
-    map_grad = lax.psum(map_terms, ("seq", "dp")) * total_tokens ** (-0.5)
+    map_grad = lax.psum(lax.psum(map_terms, "dp"), "seq") * total_tokens ** (-0.5)
     return (
         attended[None],
         dlin_queries[None],

time: 376 us -> 345 us (0.918)
  waiting for transfers between devices: 212 us -> 184 us
  local copies, waits for them, and re-layouts: 41.8 us -> 35.9 us
    psum x1 -> x2, waiting for transfers between devices: 133 us -> 105 us  [the longest x1 68.6 us: on_device(): lax.psum(lax.psum(map_terms, 'dp'), 'seq') * total_tokens ** (-0.5)]
    unnamed x75 -> x69, local copies, waits for them, and re-layouts: 18 us -> 15.8 us
  transfers between devices with their start and end apart: 7 -> 8, of which waited for: 4 -> 5; matrix products, arithmetic and copies ran while one was open for 26% -> 29% of each run, Pallas kernels for 0% -> 0%
where the time goes in v1:
time: 345 us; the launch traced here: 343 us
  waiting for transfers between devices  184 us (53%)
  matrix products  78.7 us (23%)
  local copies, waits for them, and re-layouts  35.9 us (10%)
  other arithmetic  22.5 us (7%)
  between operations  14.4 us (4%)
  starting transfers between devices  7.3 us (2%)
    all_gather x2, waiting for transfers between devices, entering(): gathered = lax.all_gather(shard.astype(jnp.bfloat16), axis)  69 us
    psum x1, waiting for transfers between devices, on_device(): lax.psum(lax.psum(map_terms, 'dp'), 'seq') * total_tokens ** (-0.5)  68.6 us
    dot_general x16, matrix products, plain(): return jnp.einsum(form, left, right, preferred_element_type=jnp.float32)  58.8 us
    psum x1, waiting for transfers between devices, on_device(): lax.psum(map_terms, 'dp')  36.7 us
    dot_general x8, matrix products, exact(): jnp.einsum(form, left.astype(jnp.float32), right.astype(jnp.float32), pre...  19.9 us
    unnamed x69, local copies, waits for them, and re-layouts  15.8 us
    ppermute x4, waiting for transfers between devices, passed_along(): return lax.ppermute(block, axis, route)  10 us
    add x7, other arithmetic, add_up(): return earlier + later  8.98 us
  transfers between devices with their start and end apart: 8, of which 5 were waited for; matrix products, arithmetic and copies ran while one was open for 29% of the time, Pallas kernels for 0%

profile of v1, /device:TPU:0, one launch (start us, length us, event | category | flops | bytes accessed | tf_op | source)
XLA Modules:
  0.0 343.5 jit_solution(16534069222115704418)
XLA Ops:
  7.2 1.2 copy.141
  8.4 1.3 copy.140
  10.4 2.8 multiply_reduce_fusion
  13.3 3.2 reverse.4
  17.7 1.4 fusion.57
  19.1 1.4 fusion.34
  20.5 69.0 %all-gather.7.cloned.1.call-done = bf16[128,128,128]{2,1,0:T(8,128)(2,1)} async-done(((bf16[16,128,128]{2,1,0:T(8,128)(2,1)}), bf16[128,128,128]{2,1,0:T(8,128)(2,1)}) %all-gather.7.cloned.1.call-update) | async-done | bytes 4194320 | tf_op jit(solution)/shard_map/all_gather | solution.py:15
  89.6 9.2 %while.23 = (s32[]{:T(128)}, f32[16,128,128]{2,1,0:T(8,128)S(1)}, s32[]{:T(128)}, bf16[8,16,128,128]{3,2,1,0:T(8,128)(2,1)}, s32[]{:T(128)}, /*index=5*/s32[]{:T(128)}, s32[]{:T(128)}, s32[]{:T(128)}) while((s32[]{:T(128)}, f32[16,128,128]{2,1,0:T(8,128)S(1)}, s32[]{:T(128)}, bf16[8,16,128,128]{3,2,1,0:T(8,128)(2,1)}, s32[]{:T(128)}, ...), condition=%wide.region_8.9_spmd, body=%wide.region_7.8_spmd.sunk | while | flops 524294 | bytes 2621575 | solution.py:22
  89.6 1.3 convert_add_fusion.5
  90.9 1.3 convert_add_fusion.5
  92.2 1.3 convert_add_fusion.5
  93.5 1.3 convert_add_fusion.5
  94.8 1.3 convert_add_fusion.5
  96.1 1.3 convert_add_fusion.5
  97.5 1.3 convert_add_fusion.5
  98.8 2.0 select_add_fusion
  100.8 2.3 fusion.14
  103.1 1.0 convolution_add_fusion.2
  104.3 1.2 fusion.41
  105.5 2.8 fusion.112
  109.5 2.0 collective-permute-start
  112.2 2.2 collective-permute-start.1
  114.4 1.2 copy.139
  115.9 5.2 %collective-permute-done = bf16[16,64,128]{2,1,0:T(8,128)(2,1)} collective-permute-done((bf16[16,64,128]{2,1,0:T(8,128)(2,1)}, bf16[16,64,128]{2,1,0:T(8,128)(2,1)}, u32[]{:S(2)}, u32[]{:S(2)}) %collective-permute-start) | collective-permute-done | bytes 262176 | tf_op jit(solution)/shard_map/ppermute | solution.py:28
  122.1 4.9 %collective-permute-done.1 = bf16[16,64,128]{2,1,0:T(8,128)(2,1)} collective-permute-done((bf16[16,64,128]{2,1,0:T(8,128)(2,1)}, bf16[16,64,128]{2,1,0:T(8,128)(2,1)}, u32[]{:S(2)}, u32[]{:S(2)}) %collective-permute-start.1) | collective-permute-done | bytes 262176 | tf_op jit(solution)/shard_map/ppermute | solution.py:28
  127.0 1.0 pad_maximum_fusion.7
  128.0 1.8 convolution_bitcast_fusion
  131.6 1.3 fusion.113
  132.9 15.4 %fusion.51 = f32[16,2,128,128]{3,2,1,0:T(8,128)} fusion(bf16[16,2,64,128]{3,2,1,0:T(8,128)(2,1)} %bitcast.171, f32[16,2,64,128]{3,2,1,0:T(8,128)} %convolution_bitcast_fusion, f32[16,2,64,128]{3,2,1,0:T(8,128)} %get-tuple-element.151, f32[16,2,64]{2,1,0:T(2,128)S(1)} %get-tuple-element.150), kind=kOutput, calls=%fused_computation.71 | convolution fusion | flops 68946048 | bytes 4726784 | tf_op jit(solution)/shard_map/hncs,hncd->hnsd/dot_general | solution.py:32
  148.3 1.8 fusion.81
  150.1 1.5 collective-permute-start.2
  151.6 7.1 %fusion.83 = f32[16,2,128,128]{3,2,1,0:T(8,128)} fusion(bf16[16,2,64,128]{3,2,1,0:T(8,128)(2,1)S(1)} %bitcast.154, f32[16,2,64]{2,1,0:T(2,128)S(1)} %get-tuple-element.150, f32[16,2,64,128]{3,2,1,0:T(8,128)} %copy-done.19, pred[2,64,128]{2,1,0:T(8,128)(4,1)S(1)} %fusion.86), kind=kOutput, calls=%fused_computation.111 | convolution fusion | flops 68421760 | bytes 3694592 | tf_op jit(solution)/shard_map/hncs,hncd->hnsd/dot_general | solution.py:32
  158.7 1.8 fusion.82
  160.5 14.2 %convolution_convert_fusion.2 = bf16[16,2,64,128]{3,2,1,0:T(8,128)(2,1)} fusion(f32[16,2,64,128]{3,2,1,0:T(8,128)} %convolution_bitcast_fusion, bf16[16,2,64,128]{3,2,1,0:T(8,128)(2,1)S(1)} %bitcast.161, bf16[16,2,64,128]{3,2,1,0:T(8,128)(2,1)} %bitcast.173, f32[16,2,64,128]{3,2,1,0:T(8,128)} %get-tuple-element.151, f32[16,2,64]{2,1,0:T(2,128)S(1)} %get-tuple-element.150), kind=kOutput, calls=%fused_computation.43 | convolution fusion | flops 71305344 | bytes 3678208 | tf_op jit(solution)/shard_map/hncs,hnsd->hncd/dot_general | solution.py:32
  174.6 1.9 slice.58
  176.5 1.3 collective-permute-start.3
  177.8 1.4 copy.114
  179.2 1.0 broadcast_in_dim_reshape.21
  180.2 1.1 slice_bitcast_fusion
  181.3 1.0 bitcast_convert_fusion.1
  182.3 1.4 fusion.49
  183.8 1.0 copy.118
  184.8 2.0 copy.127
  187.7 1.8 fusion.114
  189.5 1.1 slice.49
  190.6 1.4 convolution_select_fusion.1
  192.0 1.6 fusion.115
  193.6 2.1 fusion.4
  195.9 5.7 %fusion.17 = f32[16,2,64,128]{3,2,1,0:T(8,128)S(1)} fusion(f32[16,2,64,128]{3,2,1,0:T(8,128)} %fusion.115, bf16[16,2,64,128]{3,2,1,0:T(8,128)(2,1)S(1)} %bitcast.155, f32[1,16,128,128]{3,2,1,0:T(8,128)} %slice.49, f32[16,128,128]{2,1,0:T(8,128)S(1)} %get-tuple-element.86), kind=kOutput, calls=%fused_computation.20 | convolution fusion | flops 403963904 | bytes 4718592 | tf_op jit(solution)/shard_map/hncd,nhfd->hncf/dot_general | solution.py:36
  203.1 1.3 fusion.31
  204.8 4.0 %fusion.48 = bf16[16,2,64,128]{3,2,1,0:T(8,128)(2,1)S(1)} fusion(f32[16,2,128,128]{3,2,1,0:T(8,128)} %fusion.83, f32[16,1,64,128]{3,2,1,0:T(8,128)} %bitcast_convert_fusion, f32[16,1,64,128]{3,2,1,0:T(8,128)} %slice.58, f32[16,2,64,128]{3,2,1,0:T(8,128)} %fusion.4, f32[16,2,64,64]{3,2,1,0:T(8,128)} %convolution_select_fusion.1, ...), kind=kOutput, calls=%fused_computation.62 | convolution fusion | flops 203161600 | bytes 4718592 | tf_op jit(solution)/shard_map/hncs,hncd->hnsd/dot_general | solution.py:36
  208.8 1.1 copy.122
  209.9 2.1 broadcast_in_dim_reshape.23
  212.0 1.3 convolution_convert_fusion
  213.3 2.1 copy.126
  215.4 36.7 %all-reduce.4.cloned.1.call-done = f32[16,128,128]{1,2,0:T(8,128)} async-done(((f32[16,128,128]{1,2,0:T(8,128)}), f32[16,128,128]{1,2,0:T(8,128)}) %all-reduce.4.cloned.1.call-update) | async-done | bytes 1048592 | tf_op jit(solution)/shard_map/psum | solution.py:205
  252.1 1.3 convolution_convert_fusion.1
  253.4 2.0 copy.125
  255.5 2.5 fusion.10
  259.0 5.3 %fusion.35 = bf16[16,2,64,128]{3,2,1,0:T(8,128)(2,1)S(1)} fusion(f32[16,2,64,128]{3,2,1,0:T(8,128)S(1)} %fusion.33, bf16[16,2,64,128]{3,2,1,0:T(8,128)(2,1)S(1)} %bitcast.143, bf16[16,2,64,128]{3,2,1,0:T(8,128)(2,1)S(1)} %bitcast.169, f32[16,2,64]{2,1,0:T(2,128)S(1)} %get-tuple-element.150, f32[16,2,64,128]{3,2,1,0:T(8,128)} %copy-done.19, ...), kind=kOutput, calls=%fused_computation.40 | convolution fusion | flops 71043200 | bytes 3694592 | tf_op jit(solution)/shard_map/hncs,hnsd->hncd/dot_general | solution.py:32
  264.7 1.0 broadcast_in_dim_reshape.18
  265.7 68.6 %all-reduce.6.cloned.1.call-done = f32[16,128,128]{1,2,0:T(8,128)} async-done(((f32[16,128,128]{1,2,0:T(8,128)}), f32[16,128,128]{1,2,0:T(8,128)}) %all-reduce.6.cloned.1.call-update) | async-done | bytes 1048592 | tf_op jit(solution)/shard_map/psum | solution.py:205
  334.3 1.3 broadcast_multiply_fusion
  335.6 1.3 copy.128
  (95 shorter events, 11.3 us)
Async XLA Ops:
  7.2 2.6 copy-start
  7.2 82.3 %all-gather.7.cloned.1.call-start = ((), (), s32[]{:S(2)}) async-start(), calls=%async_computation.3 | async-start | bytes 4718592 | tf_op jit(solution)/shard_map/all_gather | solution.py:15
  8.4 1.7 copy-start.14
  10.1 3.1 copy-start.6
  13.2 182.5 %all-gather.5.cloned.1.call-start = ((), (), s32[]{:S(2)}) async-start(), calls=%async_computation.2 | async-start | bytes 4718592 | tf_op jit(solution)/shard_map/all_gather | solution.py:15
  13.3 3.2 copy-start.25
  16.5 1.1 copy-start.26
  16.6 0.8 copy-start.10
  17.7 2.8 copy-start.16
  89.6 9.2 %copy-start.28 = (pred[2]{0:T(512)(128)(4,1)S(1)}, pred[2]{0:T(512)(128)(4,1)}, u32[]{:S(2)}) copy-start(pred[2]{0:T(512)(128)(4,1)} %constant.73.clone.1) | copy-start | bytes 10
  100.8 3.4 copy-start.1
  100.8 2.3 copy-start.4
  103.1 1.2 copy-start.18
  104.2 1.4 copy-start.11
  105.5 2.8 copy-start.27
  108.3 143.8 %all-reduce.4.cloned.1.call-start = ((), (), s32[]{:S(2)}) async-start(), calls=%async_computation | async-start | bytes 2097152 | tf_op jit(solution)/shard_map/psum | solution.py:205
  109.5 11.6 %collective-permute-start = (bf16[16,64,128]{2,1,0:T(8,128)(2,1)}, bf16[16,64,128]{2,1,0:T(8,128)(2,1)}, u32[]{:S(2)}, u32[]{:S(2)}) collective-permute-start(bf16[16,64,128]{2,1,0:T(8,128)(2,1)} %get-tuple-element.134), channel_id=1, source_target_pairs={{0,4},{4,8},{8,12},{12,16},{16,20},{20,24},{24,28},{1,5},{5,9},{9,... | collective-permute-start | bytes 786440 | tf_op jit(solution)/shard_map/ppermute | solution.py:28
  112.2 14.7 %collective-permute-start.1 = (bf16[16,64,128]{2,1,0:T(8,128)(2,1)}, bf16[16,64,128]{2,1,0:T(8,128)(2,1)}, u32[]{:S(2)}, u32[]{:S(2)}) collective-permute-start(bf16[16,64,128]{2,1,0:T(8,128)(2,1)} %get-tuple-element.138), channel_id=1, source_target_pairs={{0,4},{4,8},{8,12},{12,16},{16,20},{20,24},{24,28},{1,5},{5,9},{9,... | collective-permute-start | bytes 786440 | tf_op jit(solution)/shard_map/ppermute | solution.py:28
  114.4 6.7 %copy-start.24 = (bf16[16,64,128]{2,1,0:T(8,128)(2,1)S(1)}, bf16[16,64,128]{2,1,0:T(8,128)(2,1)}, u32[]{:S(2)}) copy-start(bf16[16,64,128]{2,1,0:T(8,128)(2,1)} %get-tuple-element.135) | copy-start | bytes 786436
  115.8 14.0 %copy-start.22 = (bf16[16,128,128]{2,1,0:T(8,128)(2,1)}, bf16[16,128,128]{2,1,0:T(8,128)(2,1)S(1)}, u32[]{:S(2)}) copy-start(bf16[16,128,128]{2,1,0:T(8,128)(2,1)S(1)} %copy.106) | copy-start | bytes 1572868
  122.1 8.5 %copy-start.23 = (bf16[16,128,128]{2,1,0:T(8,128)(2,1)}, bf16[16,128,128]{2,1,0:T(8,128)(2,1)S(1)}, u32[]{:S(2)}) copy-start(bf16[16,128,128]{2,1,0:T(8,128)(2,1)S(1)} %pad_maximum_fusion.6) | copy-start | bytes 1572868
  127.9 1.8 copy-start.20
  130.6 1.0 copy-start.19
  150.1 31.2 %collective-permute-start.2 = (bf16[16,64,128]{2,1,0:T(8,128)(2,1)}, bf16[16,64,128]{2,1,0:T(8,128)(2,1)}, u32[]{:S(2)}, u32[]{:S(2)}) collective-permute-start(bf16[16,64,128]{2,1,0:T(8,128)(2,1)} %fusion.81), channel_id=1, source_target_pairs={{4,0},{8,4},{12,8},{16,12},{20,16},{24,20},{28,24},{5,1},{9,5},{13... | collective-permute-start | bytes 786440 | tf_op jit(solution)/shard_map/ppermute | solution.py:28
  176.5 10.3 %collective-permute-start.3 = (bf16[16,64,128]{2,1,0:T(8,128)(2,1)}, bf16[16,64,128]{2,1,0:T(8,128)(2,1)S(1)}, u32[]{:S(2)}, u32[]{:S(2)}) collective-permute-start(bf16[16,64,128]{2,1,0:T(8,128)(2,1)} %fusion.82), channel_id=1, source_target_pairs={{4,0},{8,4},{12,8},{16,12},{20,16},{24,20},{28,24},{5,1},{9,5},{13... | collective-permute-start | bytes 786440 | tf_op jit(solution)/shard_map/ppermute | solution.py:28
  189.5 2.5 copy-start.5
  190.6 3.0 copy-start.2
  195.8 5.7 %copy-start.7 = (f32[16,128,128]{2,1,0:T(8,128)S(1)}, f32[16,128,128]{2,1,0:T(8,128)}, u32[]{:S(2)}) copy-start(f32[16,128,128]{2,1,0:T(8,128)} %copy-done.6) | copy-start | bytes 3145732
  201.6 1.1 copy-start.15
  201.6 1.5 copy-start.8
  201.6 1.5 copy-start.17
  201.9 0.8 copy-start.12
  204.5 129.8 %all-reduce.6.cloned.1.call-start = ((), (), s32[]{:S(2)}) async-start(), calls=%async_computation.1 | async-start | bytes 2097152 | tf_op jit(solution)/shard_map/psum | solution.py:205
  208.8 3.2 copy-start.9
  213.3 38.9 %copy-start.13 = (bf16[16,128,128]{2,1,0:T(8,128)(2,1)S(1)}, bf16[16,128,128]{2,1,0:T(8,128)(2,1)}, u32[]{:S(2)}) copy-start(bf16[16,128,128]{2,1,0:T(8,128)(2,1)} %copy-done.12) | copy-start | bytes 1572868
  255.5 2.5 copy-start.3
  258.0 1.0 copy-start.21
Sparse Core Ops, SparseCore 0:
  13.3 76.0 all-gather.6
  108.4 81.4 all-gather.4
  204.6 47.4 all-reduce.3
  255.9 78.3 all-reduce.5
